TPU v7x, 32 devices: a whole 2x2x4 slice. The times are simulated.
32 devices in a mesh: tier: 4 (over x, core), tile: 8 (over z, y).
Axes of the slice: x: 2, y: 2, z: 4, core: 2. Of those that a mesh axis runs over, the one named last changes fastest.
Arguments:
- starting_warmth_rise: float32 [32, 96, 1024], P('tile', 'tier'), may hold values from -3 to 8
- substance_per_cell: int32 [32, 96, 1024], P('tile', 'tier'), may hold values from 0 to 7
- material_transport_rates: float32 [2, 8], replicated, may hold values from 0.2 to 2
- patch_region_label: int32 [8, 8], P('tile'), may hold values from 0 to 15, as said below
- static_power_per_area: float32 [4, 16], replicated, may hold values from 0.5 to 4
- warming_power_factor: float32 [4, 16], replicated, may hold values from 0.2 to 0.8
- stacking_solve_operator: float32 [96, 96], replicated, may hold values from 0 to 1
Outputs:
- final_temperature: float32 [32, 96, 1024], P('tile', 'tier')
- block_power: float32 [4, 16], P('tier')
Inputs may be any that keep to these rules, and one draw needn't show every extreme that they name: `patch_region_label`: every block number names at least one tile.
All inputs are finite; a program needn't handle non-finite values.
Results may differ from a plain program's by a relative error of at most 0.0001.
Values sent between devices are 32-bit elements; how exact they have to be, the bound alone decides.
A program may use at most 64 MiB of HBM per device.

v0:
```python
import jax
import jax.numpy as jnp
from jax import lax
from jax.sharding import PartitionSpec as P

TILE_COLS = 128
STEPS = 2
LATERAL_RATE = 0.12
SOURCE_GAIN = 0.02


def extended(block, sides, width):
    for axis, dim in sides:
        count = lax.axis_size(axis)
        forward = [(i, i + 1) for i in range(count - 1)]
        backward = [(target, source) for source, target in forward]
        low = lax.ppermute(
            lax.slice_in_dim(block, block.shape[dim] - width, None, axis=dim), axis, forward
        )
        high = lax.ppermute(lax.slice_in_dim(block, 0, width, axis=dim), axis, backward)
        block = jnp.concatenate([low, block, high], axis=dim)
    return block


def pair_mean(cond_a, cond_b):
    return 2.0 * cond_a * cond_b / (cond_a + cond_b)


def lateral(padded, conduct):
    centre = padded[1:-1, :, 1:-1]
    sideways_coupling_rate = conduct[0, 1:-1, :, 1:-1]
    stacking_coupling_rate = conduct[1, 1:-1, :, 1:-1]
    flow_sum = pair_mean(sideways_coupling_rate, conduct[0, 2:, :, 1:-1]) * (
        padded[2:, :, 1:-1] - centre
    )
    flow_sum = flow_sum + pair_mean(sideways_coupling_rate, conduct[0, :-2, :, 1:-1]) * (
        padded[:-2, :, 1:-1] - centre
    )
    flow_sum = flow_sum + pair_mean(stacking_coupling_rate, conduct[1, 1:-1, :, 2:]) * (
        padded[1:-1, :, 2:] - centre
    )
    flow_sum = flow_sum + pair_mean(stacking_coupling_rate, conduct[1, 1:-1, :, :-2]) * (
        padded[1:-1, :, :-2] - centre
    )
    return centre + LATERAL_RATE * flow_sum


def exact_dot(left_op, right_op):
    return jnp.dot(
        left_op, right_op, precision=lax.Precision.HIGHEST, preferred_element_type=jnp.float32
    )


def lookup_codes(codes, material_transport_rates):
    sideways_coupling_rate = jnp.zeros(codes.shape, jnp.float32)
    stacking_coupling_rate = jnp.zeros(codes.shape, jnp.float32)
    for material in range(material_transport_rates.shape[1]):
        is_material = codes == material + 1
        sideways_coupling_rate = jnp.where(
            is_material, material_transport_rates[0, material], sideways_coupling_rate
        )
        stacking_coupling_rate = jnp.where(
            is_material, material_transport_rates[1, material], stacking_coupling_rate
        )
    return jnp.stack([sideways_coupling_rate, stacking_coupling_rate])


def tile_partials(active, tile_hot):
    mesh_height_cells, groups, col_count = active.shape
    quarter = col_count // TILE_COLS
    tile_sums = active.reshape(mesh_height_cells, groups, quarter, TILE_COLS).sum(axis=(0, 3))
    partial_value = exact_dot(tile_sums, tile_hot)
    counts = float(mesh_height_cells * TILE_COLS) * jnp.sum(tile_hot, axis=0)
    return (partial_value, counts)


def spread_power(block_power, tile_hot, mesh_height_cells):
    tile_power = exact_dot(block_power, tile_hot.T)
    groups, quarter = tile_power.shape
    cells = jnp.broadcast_to(
        tile_power[None, :, :, None], (mesh_height_cells, groups, quarter, TILE_COLS)
    )
    return cells.reshape(mesh_height_cells, groups, quarter * TILE_COLS)


def leak_tiers(active, tile_hot, static_power_per_area, warming_power_factor, tier_id):
    partial_value, counts = tile_partials(active, tile_hot)
    block_sum, block_count = lax.psum((partial_value[0], counts), "tile")
    base_row = lax.dynamic_slice_in_dim(static_power_per_area, tier_id, 1, 0)
    slope_row = lax.dynamic_slice_in_dim(warming_power_factor, tier_id, 1, 0)
    return base_row * jnp.exp(slope_row * block_sum[None, :] / block_count[None, :])


def shards(
    starting_warmth_rise,
    substance_per_cell,
    material_transport_rates,
    patch_region_label,
    static_power_per_area,
    warming_power_factor,
    stacking_solve_operator,
):
    mesh_height_cells, stacked_layer_number, lateral_width_cells = starting_warmth_rise.shape
    tier_id = lax.axis_index("tier")
    block_total = static_power_per_area.shape[1]
    codes = substance_per_cell + 1
    block_range = jnp.arange(block_total, dtype=jnp.int32)
    cond_pad = extended(lookup_codes(codes, material_transport_rates), (("tile", 1),), 1)
    cond_pad = jnp.pad(cond_pad, ((0, 0), (0, 0), (0, 0), (1, 1)))
    tile_hot = (patch_region_label[0][:, None] == block_range[None, :]).astype(jnp.float32)
    present_warming_state = starting_warmth_rise
    power_row = jnp.zeros((1, block_total), jnp.float32)
    for step_index in range(STEPS):
        padded = extended(present_warming_state, (("tile", 0),), 1)
        padded = jnp.pad(padded, ((0, 0), (0, 0), (1, 1)))
        power_row = leak_tiers(
            present_warming_state[:, ::stacked_layer_number, :],
            tile_hot,
            static_power_per_area,
            warming_power_factor,
            tier_id,
        )
        moved_field = lateral(padded, cond_pad)
        moved_field = moved_field.at[:, ::stacked_layer_number, :].add(
            SOURCE_GAIN * spread_power(power_row, tile_hot, mesh_height_cells)
        )
        applied = jnp.einsum(
            "lm,rmc->rlc",
            stacking_solve_operator,
            lax.all_to_all(moved_field, "tier", split_axis=2, concat_axis=1, tiled=True),
            precision=lax.Precision.HIGHEST,
        )
        present_warming_state = lax.all_to_all(
            applied, "tier", split_axis=1, concat_axis=2, tiled=True
        )
    return (present_warming_state, power_row)


def solution(mesh):
    in_specs = (
        P("tile", "tier", None),
        P("tile", "tier", None),
        P(),
        P("tile", None),
        P(),
        P(),
        P(),
    )
    out_specs = (P("tile", "tier", None), P("tier", None))
    return jax.shard_map(shards, mesh=mesh, in_specs=in_specs, out_specs=out_specs, check_vma=False)
```

profile of v0, /device:TPU:8, one launch (start us, length us, event | category | flops | bytes accessed | tf_op | source)
XLA Modules:
  0.0 144.2 jit_solution(3918848064363869905)
XLA Ops:
  0.6 1.0 fusion.41
  1.6 3.4 %collective-permute-start.3 = (f32[1,24,1024]{2,1,0:T(8,128)S(1)}, f32[1,24,1024]{2,1,0:T(8,128)S(1)}, u32[]{:S(2)}, u32[]{:S(2)}) collective-permute-start(f32[1,24,1024]{2,1,0:T(8,128)S(1)} %get-tuple-element.44), channel_id=1, source_target_pairs={{0,1},{1,2},{2,3},{3,4},{4,5},{5,6},{6,7},{8,9},{9,10},{10,11},{11... | collective-permute-start | bytes 294920 | tf_op jit(solution)/shard_map/ppermute | solution.py:17
  5.0 3.3 %collective-permute-start.1 = (f32[1,24,1024]{2,1,0:T(8,128)S(1)}, f32[1,24,1024]{2,1,0:T(8,128)S(1)}, u32[]{:S(2)}, u32[]{:S(2)}) collective-permute-start(f32[1,24,1024]{2,1,0:T(8,128)S(1)} %get-tuple-element.45), channel_id=1, source_target_pairs={{1,0},{2,1},{3,2},{4,3},{5,4},{6,5},{7,6},{9,8},{10,9},{11,10},{12... | collective-permute-start | bytes 294920 | tf_op jit(solution)/shard_map/ppermute | solution.py:20
  8.4 2.0 %fusion.42 = (f32[1,1]{1,0:T(1,128)}, f32[1,1]{1,0:T(1,128)}, f32[1,1]{1,0:T(1,128)}, f32[1,1]{1,0:T(1,128)}, f32[1,1]{1,0:T(1,128)}, /*index=5*/f32[1,1]{1,0:T(...) fusion(f32[2,8]{1,0:T(2,128)} %param.13), kind=kLoop, calls=%fused_computation.105 | loop fusion | bytes 128 | tf_op jit(solution)/shard_map/slice | solution.py:60
  10.3 6.6 %select_select_fusion = (f32[4,24,1024]{2,1,0:T(8,128)S(1)}, pred[4,24,1024]{2,1,0:T(8,128)(4,1)S(1)}, pred[4,24,1024]{2,1,0:T(8,128)(4,1)S(1)}, pred[4,24,1024]...) fusion(f32[]{:T(128)} %bitcast.16, f32[]{:T(128)} %bitcast.15, ...), kind=kLoop, calls=%fused_computation.62 | loop fusion | flops 1671168 | bytes 1572896 | tf_op jit(solution)/shard_map/jit(_where)/select_n | solution.py:62
  17.0 5.4 %select_select_fusion.1 = f32[4,24,1024]{2,1,0:T(8,128)S(1)} fusion(pred[4,24,1024]{2,1,0:T(8,128)(4,1)S(1)} %get-tuple-element.39, pred[4,24,1024]{2,1,0:T(8,128)(4,1)S(1)} %get-tuple-element.38, pred[4,24,1024]{2,1,0:T(8,128)(4,1)S(1)} %get-tuple-element.37, pred[4,24,1024]{2,1,0:T(8,128)(4,1)S(1)} %get-tuple-element.36, ...), kind=kLoop, calls=%fused_computation.63 | loop fusion | flops 786432 | bytes 1179680 | tf_op jit(solution)/shard_map/jit(_where)/select_n | solution.py:59
  22.4 2.5 %collective-permute-start.2 = (f32[2,1,24,1024]{3,2,1,0:T(8,128)S(1)}, f32[2,1,24,1024]{3,2,1,0:T(8,128)S(1)}, u32[]{:S(2)}, u32[]{:S(2)}) collective-permute-start(f32[2,1,24,1024]{3,2,1,0:T(8,128)S(1)} %get-tuple-element.40), channel_id=1, source_target_pairs={{0,1},{1,2},{2,3},{3,4},{4,5},{5,6},{6,7},{8,9},{9,10},{10,11},{11... | collective-permute-start | bytes 589832 | tf_op jit(solution)/shard_map/ppermute | solution.py:17
  24.9 4.2 %collective-permute-start = (f32[2,1,24,1024]{3,2,1,0:T(8,128)S(1)}, f32[2,1,24,1024]{3,2,1,0:T(8,128)S(1)}, u32[]{:S(2)}, u32[]{:S(2)}) collective-permute-start(f32[2,1,24,1024]{3,2,1,0:T(8,128)S(1)} %get-tuple-element.41), channel_id=1, source_target_pairs={{1,0},{2,1},{3,2},{4,3},{5,4},{6,5},{7,6},{9,8},{10,9},{11,10},{12... | collective-permute-start | bytes 589832 | tf_op jit(solution)/shard_map/ppermute | solution.py:20
  29.6 17.1 %all-reduce.3 = (f32[1,16]{1,0:T(1,128)S(1)}, f32[1,16]{1,0:T(1,128)S(1)}) all-reduce(f32[1,16]{1,0:T(1,128)S(1)} %multiply_bitcast_fusion.2, f32[1,16]{1,0:T(1,128)S(1)} %fusion.31), channel_id=1, replica_groups=mesh['tier'=4,'tile'=8] {'tile'}, use_global_device_ids=true, to_apply=%region_4.5 | all-reduce | flops 32 | bytes 256 | tf_op jit(solution)/shard_map/psum | solution.py:88
  47.6 1.2 fusion.18
  49.0 0.9 copy.88
  49.9 2.9 %reshape.124 = f32[4,1,24576]{2,1,0:T(1,128)S(1)} reshape(f32[1024,4,24]{2,1,0:T(4,128)S(1)} %bitcast.115) | data formatting | bytes 786432
  52.8 10.0 %all_to_all.72 = f32[4,1,24576]{2,1,0:T(1,128)S(1)} all-to-all(f32[4,1,24576]{2,1,0:T(1,128)S(1)} %reshape.124), channel_id=1, replica_groups=mesh['tier'=4,'tile'=8] {'tier'}, dimensions={0} | all-to-all | bytes 786432 | tf_op jit(solution)/shard_map/all_to_all | solution.py:130
  62.8 0.5 broadcast.157
  63.3 1.7 %reduce.10 = f32[4,24576]{1,0:T(4,128)S(1)} reduce(f32[4,1,24576]{2,1,0:T(1,128)S(1)} %all_to_all.72, f32[]{:T(128)} %broadcast.157), dimensions={1}, to_apply=%all_to_all.52.reduce_sub_computation | reduce | bytes 786436 | tf_op jit(solution)/shard_map/all_to_all | solution.py:130
  65.0 2.8 %reshape.125 = f32[1024,4,24]{2,1,0:T(4,128)S(1)} reshape(f32[4,24576]{1,0:T(4,128)S(1)} %reduce.10) | data formatting | bytes 786432
  67.8 0.8 copy.89
  69.4 9.8 %all_to_all.73 = f32[4,96,256]{2,0,1:T(4,128)S(1)} all-to-all(f32[4,96,256]{2,0,1:T(4,128)S(1)} %copy.90), channel_id=1, replica_groups=mesh['tier'=4,'tile'=8] {'tier'}, dimensions={1} | all-to-all | bytes 786432 | tf_op jit(solution)/shard_map/all_to_all | solution.py:133
  80.1 17.1 %psum.26 = f32[1,16]{1,0:T(1,128)S(1)} all-reduce(f32[1,16]{1,0:T(1,128)S(1)} %fusion.30), channel_id=1, replica_groups=mesh['tier'=4,'tile'=8] {'tile'}, use_global_device_ids=true, to_apply=%region_7.8 | all-reduce | flops 16 | bytes 128 | tf_op jit(solution)/shard_map/psum | solution.py:88
  97.5 6.6 %collective-permute-start.4 = (f32[1,24,1024]{2,1,0:T(8,128)S(1)}, f32[1,24,1024]{2,1,0:T(8,128)S(1)}, u32[]{:S(2)}, u32[]{:S(2)}) collective-permute-start(f32[1,24,1024]{2,1,0:T(8,128)S(1)} %slice.219), channel_id=1, source_target_pairs={{1,0},{2,1},{3,2},{4,3},{5,4},{6,5},{7,6},{9,8},{10,9},{11,10},{12... | collective-permute-start | bytes 294920 | tf_op jit(solution)/shard_map/ppermute | solution.py:20
  104.1 1.9 %collective-permute-start.5 = (f32[1,24,1024]{2,1,0:T(8,128)S(1)}, f32[1,24,1024]{2,1,0:T(8,128)S(1)}, u32[]{:S(2)}, u32[]{:S(2)}) collective-permute-start(f32[1,24,1024]{2,1,0:T(8,128)S(1)} %slice.222), channel_id=1, source_target_pairs={{0,1},{1,2},{2,3},{3,4},{4,5},{5,6},{6,7},{8,9},{9,10},{10,11},{11... | collective-permute-start | bytes 294920 | tf_op jit(solution)/shard_map/ppermute | solution.py:17
  106.3 5.2 %collective-permute-done.5 = f32[1,24,1024]{2,1,0:T(8,128)S(1)} collective-permute-done((f32[1,24,1024]{2,1,0:T(8,128)S(1)}, f32[1,24,1024]{2,1,0:T(8,128)S(1)}, u32[]{:S(2)}, u32[]{:S(2)}) %collective-permute-start.5) | collective-permute-done | bytes 98336 | tf_op jit(solution)/shard_map/ppermute | solution.py:17
  111.8 1.4 fusion.7
  113.5 0.9 copy.92
  114.4 2.9 %reshape.126 = f32[4,1,24576]{2,1,0:T(1,128)S(1)} reshape(f32[1024,4,24]{2,1,0:T(4,128)S(1)} %bitcast.117) | data formatting | bytes 786432
  117.3 9.8 %all_to_all.74 = f32[4,1,24576]{2,1,0:T(1,128)S(1)} all-to-all(f32[4,1,24576]{2,1,0:T(1,128)S(1)} %reshape.126), channel_id=1, replica_groups=mesh['tier'=4,'tile'=8] {'tier'}, dimensions={0} | all-to-all | bytes 786432 | tf_op jit(solution)/shard_map/all_to_all | solution.py:130
  127.1 1.7 %reduce.11 = f32[4,24576]{1,0:T(4,128)S(1)} reduce(f32[4,1,24576]{2,1,0:T(1,128)S(1)} %all_to_all.74, f32[]{:T(128)} %broadcast.157), dimensions={1}, to_apply=%all_to_all.60.reduce_sub_computation | reduce | bytes 786436 | tf_op jit(solution)/shard_map/all_to_all | solution.py:130
  128.8 2.8 %reshape.127 = f32[1024,4,24]{2,1,0:T(4,128)S(1)} reshape(f32[4,24576]{1,0:T(4,128)S(1)} %reduce.11) | data formatting | bytes 786432
  131.6 0.8 copy.93
  132.4 0.5 convolution_bitcast_fusion
  133.2 9.8 %all_to_all.75 = f32[4,96,256]{2,0,1:T(4,128)S(1)} all-to-all(f32[4,96,256]{2,0,1:T(4,128)S(1)} %copy.94), channel_id=1, replica_groups=mesh['tier'=4,'tile'=8] {'tier'}, dimensions={1} | all-to-all | bytes 786432 | tf_op jit(solution)/shard_map/all_to_all | solution.py:133
  143.3 0.9 all_to_all.67
  (51 shorter events, 4.8 us)
Async XLA Ops:
  0.6 68.0 %copy-start = (f32[96,96]{1,0:T(8,128)S(1)}, f32[96,96]{1,0:T(8,128)}, u32[]{:S(2)}) copy-start(f32[96,96]{1,0:T(8,128)} %param.17) | copy-start | bytes 110596
  1.6 45.3 %collective-permute-start.3 = (f32[1,24,1024]{2,1,0:T(8,128)S(1)}, f32[1,24,1024]{2,1,0:T(8,128)S(1)}, u32[]{:S(2)}, u32[]{:S(2)}) collective-permute-start(f32[1,24,1024]{2,1,0:T(8,128)S(1)} %get-tuple-element.44), channel_id=1, source_target_pairs={{0,1},{1,2},{2,3},{3,4},{4,5},{5,6},{6,7},{8,9},{9,10},{10,11},{11... | collective-permute-start | bytes 294920 | tf_op jit(solution)/shard_map/ppermute | solution.py:17
  5.0 41.9 %collective-permute-start.1 = (f32[1,24,1024]{2,1,0:T(8,128)S(1)}, f32[1,24,1024]{2,1,0:T(8,128)S(1)}, u32[]{:S(2)}, u32[]{:S(2)}) collective-permute-start(f32[1,24,1024]{2,1,0:T(8,128)S(1)} %get-tuple-element.45), channel_id=1, source_target_pairs={{1,0},{2,1},{3,2},{4,3},{5,4},{6,5},{7,6},{9,8},{10,9},{11,10},{12... | collective-permute-start | bytes 294920 | tf_op jit(solution)/shard_map/ppermute | solution.py:20
  16.9 12.2 %copy-start.3 = (f32[4,24,1024]{2,1,0:T(8,128)S(1)}, f32[4,24,1024]{2,1,0:T(8,128)}, u32[]{:S(2)}) copy-start(f32[4,24,1024]{2,1,0:T(8,128)} %param.11) | copy-start | bytes 1179652
  16.9 12.2 %copy-start.7 = (s32[1,8]{1,0:T(1,128)S(1)}, s32[1,8]{1,0:T(1,128)}, u32[]{:S(2)}) copy-start(s32[1,8]{1,0:T(1,128)} %param.14) | copy-start | bytes 100
  16.9 29.7 %copy-start.5 = (f32[4,16]{1,0:T(4,128)S(1)}, f32[4,16]{1,0:T(4,128)}, u32[]{:S(2)}) copy-start(f32[4,16]{1,0:T(4,128)} %param.15) | copy-start | bytes 772
  16.9 29.7 %copy-start.6 = (f32[4,16]{1,0:T(4,128)S(1)}, f32[4,16]{1,0:T(4,128)}, u32[]{:S(2)}) copy-start(f32[4,16]{1,0:T(4,128)} %param.16) | copy-start | bytes 772
  22.4 24.8 %collective-permute-start.2 = (f32[2,1,24,1024]{3,2,1,0:T(8,128)S(1)}, f32[2,1,24,1024]{3,2,1,0:T(8,128)S(1)}, u32[]{:S(2)}, u32[]{:S(2)}) collective-permute-start(f32[2,1,24,1024]{3,2,1,0:T(8,128)S(1)} %get-tuple-element.40), channel_id=1, source_target_pairs={{0,1},{1,2},{2,3},{3,4},{4,5},{5,6},{6,7},{8,9},{9,10},{10,11},{11... | collective-permute-start | bytes 589832 | tf_op jit(solution)/shard_map/ppermute | solution.py:17
  24.9 22.3 %collective-permute-start = (f32[2,1,24,1024]{3,2,1,0:T(8,128)S(1)}, f32[2,1,24,1024]{3,2,1,0:T(8,128)S(1)}, u32[]{:S(2)}, u32[]{:S(2)}) collective-permute-start(f32[2,1,24,1024]{3,2,1,0:T(8,128)S(1)} %get-tuple-element.41), channel_id=1, source_target_pairs={{1,0},{2,1},{3,2},{4,3},{5,4},{6,5},{7,6},{9,8},{10,9},{11,10},{12... | collective-permute-start | bytes 589832 | tf_op jit(solution)/shard_map/ppermute | solution.py:20
  47.6 1.3 copy-start.1
  79.5 32.3 %copy-start.2 = (f32[2,6,24,1026]{3,2,1,0:T(8,128)S(1)}, f32[2,6,24,1026]{3,2,1,0:T(8,128)}, u32[]{:S(2)}) copy-start(f32[2,6,24,1026]{3,2,1,0:T(8,128)} %copy-done.1) | copy-start | bytes 3545860
  97.2 16.0 %copy-start.4 = (f32[1,16]{1,0:T(1,128)}, f32[1,16]{1,0:T(1,128)S(1)}, u32[]{:S(2)}) copy-start(f32[1,16]{1,0:T(1,128)S(1)} %exponential_multiply_fusion) | copy-start | bytes 196
  97.5 8.8 %collective-permute-start.4 = (f32[1,24,1024]{2,1,0:T(8,128)S(1)}, f32[1,24,1024]{2,1,0:T(8,128)S(1)}, u32[]{:S(2)}, u32[]{:S(2)}) collective-permute-start(f32[1,24,1024]{2,1,0:T(8,128)S(1)} %slice.219), channel_id=1, source_target_pairs={{1,0},{2,1},{3,2},{4,3},{5,4},{6,5},{7,6},{9,8},{10,9},{11,10},{12... | collective-permute-start | bytes 294920 | tf_op jit(solution)/shard_map/ppermute | solution.py:20
  104.1 7.4 %collective-permute-start.5 = (f32[1,24,1024]{2,1,0:T(8,128)S(1)}, f32[1,24,1024]{2,1,0:T(8,128)S(1)}, u32[]{:S(2)}, u32[]{:S(2)}) collective-permute-start(f32[1,24,1024]{2,1,0:T(8,128)S(1)} %slice.222), channel_id=1, source_target_pairs={{0,1},{1,2},{2,3},{3,4},{4,5},{5,6},{6,7},{8,9},{9,10},{10,11},{11... | collective-permute-start | bytes 294920 | tf_op jit(solution)/shard_map/ppermute | solution.py:17
where the time goes:
time: 145 us; the launch traced here: 144 us
  blocking collectives  73.7 us (51%)
  starting transfers between devices  22 us (15%)
  local copies, waits for them, and re-layouts  21 us (14%)
  other arithmetic  19.3 us (13%)
  waiting for transfers between devices  5.42 us (4%)
  matrix products  1.71 us (1%)
    psum x2, blocking collectives, leak_tiers(): block_sum, block_count = lax.psum((partial_value[0], counts), 'tile')  34.2 us
    all_to_all x2, blocking collectives, shards(): lax.all_to_all(moved_field, 'tier', split_axis=2, concat_axis=1, tiled=True)  19.8 us
    all_to_all x2, blocking collectives, shards(): lax.all_to_all(applied, 'tier', split_axis=1, concat_axis=2, tiled=True)  19.7 us
    ppermute x3, starting transfers between devices, extended(): lax.ppermute(lax.slice_in_dim(block, 0, width, axis=dim), axis, backward)  14.1 us
    unnamed x20, local copies, waits for them, and re-layouts  11.4 us
    ppermute x3, starting transfers between devices, extended(): lax.ppermute(lax.slice_in_dim(block, block.shape[dim] - width, None, axis...  7.88 us
    select_n x1, other arithmetic, lookup_codes(): jnp.where(is_material, material_transport_rates[1, material], stacking_co...  6.55 us
    select_n x1, other arithmetic, lookup_codes(): jnp.where(is_material, material_transport_rates[0, material], sideways_co...  5.36 us
  transfers between devices with their start and end apart: 6, of which 2 were waited for; matrix products, arithmetic and copies ran while one was open for 10% of the time, Pallas kernels for 0%

commit v1 on v0

--- a/solution.py
+++ b/solution.py
@@ -2,11 +2,44 @@
 import jax.numpy as jnp
 from jax import lax
 from jax.sharding import PartitionSpec as P
+from jax.lax import axis_index, axis_size, ppermute
 
 TILE_COLS = 128
 STEPS = 2
 LATERAL_RATE = 0.12
 SOURCE_GAIN = 0.02
+
+
+def bring_view_on(u, at_axis, mat):
+    block_now, d_next = (u.shape[:at_axis], u.shape[at_axis + 1 :])
+    formed = u.reshape(*block_now, mat, -1, *d_next)
+    block_last = jnp.moveaxis(formed, at_axis, 0)
+    return block_last
+
+
+def clear_the_tracks(here_x, array_dim):
+    here_x = jnp.moveaxis(here_x, 0, array_dim)
+    f_now = here_x.shape
+    local_out = here_x.reshape(
+        *f_now[:array_dim], f_now[array_dim] * f_now[array_dim + 1], *f_now[array_dim + 2 :]
+    )
+    return local_out
+
+
+def ranges_unite(body, which_axis, own_rows, my_data):
+    clean = axis_index(which_axis)
+    shaped = axis_size(which_axis)
+    work_now, right_arr = (shaped, clean)
+    m_next = bring_view_on(body, own_rows, work_now)
+    queue = [m_next[right_arr]]
+    for i0 in range(1, work_now):
+        fresh = m_next[right_arr ^ i0]
+        f_next = ppermute(fresh, which_axis, [(j, j ^ i0) for j in range(work_now)])
+        queue.append(f_next)
+    u1 = jnp.stack(queue)
+    m_next = u1[right_arr ^ jnp.arange(work_now)]
+    tile_out = clear_the_tracks(m_next, my_data)
+    return tile_out
 
 
 def extended(block, sides, width):
@@ -130,9 +163,7 @@
             lax.all_to_all(moved_field, "tier", split_axis=2, concat_axis=1, tiled=True),
             precision=lax.Precision.HIGHEST,
         )
-        present_warming_state = lax.all_to_all(
-            applied, "tier", split_axis=1, concat_axis=2, tiled=True
-        )
+        present_warming_state = ranges_unite(applied, "tier", 1, 2)
     return (present_warming_state, power_row)
 
 

time: 145 us -> 135 us (0.931)
  the two profiles are of different devices: /device:TPU:8 before, /device:TPU:0 now
where the time goes in v1:
time: 135 us; the launch traced here: 134 us
  blocking collectives  47.2 us (35%)
  starting transfers between devices  26.8 us (20%)
  local copies, waits for them, and re-layouts  20.6 us (15%)
  other arithmetic  19.1 us (14%)
  waiting for transfers between devices  17.4 us (13%)
  matrix products  1.71 us (1%)
    psum x2, blocking collectives, leak_tiers(): block_sum, block_count = lax.psum((partial_value[0], counts), 'tile')  37.4 us
    ppermute x3, starting transfers between devices, extended(): lax.ppermute(lax.slice_in_dim(block, block.shape[dim] - width, None, axis...  15.5 us
    unnamed x21, local copies, waits for them, and re-layouts  12.1 us
    ppermute x6, waiting for transfers between devices, ranges_unite(): f_next = ppermute(fresh, which_axis, [(j, j ^ i0) for j in range(work_now)])  9.99 us
    all_to_all x1, blocking collectives, shards(): lax.all_to_all(moved_field, 'tier', split_axis=2, concat_axis=1, tiled=True)  9.84 us
    all_to_all x1, waiting for transfers between devices, shards(): lax.all_to_all(moved_field, 'tier', split_axis=2, concat_axis=1, tiled=True)  7.38 us
    select_n x1, other arithmetic, lookup_codes(): jnp.where(is_material, material_transport_rates[1, material], stacking_co...  6.46 us
    select_n x1, other arithmetic, lookup_codes(): jnp.where(is_material, material_transport_rates[0, material], sideways_co...  5.32 us
  transfers between devices with their start and end apart: 13, of which 5 were waited for; matrix products, arithmetic and copies ran while one was open for 1% of the time, Pallas kernels for 0%

profile of v1, /device:TPU:0, one launch (start us, length us, event | category | flops | bytes accessed | tf_op | source)
XLA Modules:
  0.0 133.9 jit_solution(5757139597803868348)
XLA Ops:
  0.6 2.0 %fusion.44 = (f32[1,1]{1,0:T(1,128)}, f32[1,1]{1,0:T(1,128)}, f32[1,1]{1,0:T(1,128)}, f32[1,1]{1,0:T(1,128)}, f32[1,1]{1,0:T(1,128)}, /*index=5*/f32[1,1]{1,0:T(...) fusion(f32[2,8]{1,0:T(2,128)} %param.13), kind=kLoop, calls=%fused_computation.120 | loop fusion | bytes 128 | tf_op jit(solution)/shard_map/slice | solution.py:93
  2.6 6.5 %select_select_fusion = (f32[4,24,1024]{2,1,0:T(8,128)S(1)}, pred[4,24,1024]{2,1,0:T(8,128)(4,1)S(1)}, pred[4,24,1024]{2,1,0:T(8,128)(4,1)S(1)}, pred[4,24,1024]...) fusion(f32[]{:T(128)} %bitcast.16, f32[]{:T(128)} %bitcast.15, ...), kind=kLoop, calls=%fused_computation.63 | loop fusion | flops 1671168 | bytes 1572896 | tf_op jit(solution)/shard_map/jit(_where)/select_n | solution.py:95
  9.1 5.3 %select_select_fusion.1 = f32[4,24,1024]{2,1,0:T(8,128)S(1)} fusion(pred[4,24,1024]{2,1,0:T(8,128)(4,1)S(1)} %get-tuple-element.39, pred[4,24,1024]{2,1,0:T(8,128)(4,1)S(1)} %get-tuple-element.38, pred[4,24,1024]{2,1,0:T(8,128)(4,1)S(1)} %get-tuple-element.37, pred[4,24,1024]{2,1,0:T(8,128)(4,1)S(1)} %get-tuple-element.36, ...), kind=kLoop, calls=%fused_computation.64 | loop fusion | flops 786432 | bytes 1179680 | tf_op jit(solution)/shard_map/jit(_where)/select_n | solution.py:92
  14.5 1.3 collective-permute-start
  15.8 5.5 %collective-permute-start.2 = (f32[2,1,24,1024]{3,2,1,0:T(8,128)S(1)}, f32[2,1,24,1024]{3,2,1,0:T(8,128)S(1)}, u32[]{:S(2)}, u32[]{:S(2)}) collective-permute-start(f32[2,1,24,1024]{3,2,1,0:T(8,128)S(1)} %get-tuple-element.40), channel_id=1, source_target_pairs={{0,1},{1,2},{2,3},{3,4},{4,5},{5,6},{6,7},{8,9},{9,10},{10,11},{11... | collective-permute-start | bytes 589832 | tf_op jit(solution)/shard_map/ppermute | solution.py:50
  21.4 1.3 collective-permute-start.1
  22.7 5.4 %collective-permute-start.3 = (f32[1,24,1024]{2,1,0:T(8,128)S(1)}, f32[1,24,1024]{2,1,0:T(8,128)S(1)}, u32[]{:S(2)}, u32[]{:S(2)}) collective-permute-start(f32[1,24,1024]{2,1,0:T(8,128)S(1)} %get-tuple-element.52), channel_id=1, source_target_pairs={{0,1},{1,2},{2,3},{3,4},{4,5},{5,6},{6,7},{8,9},{9,10},{10,11},{11... | collective-permute-start | bytes 294920 | tf_op jit(solution)/shard_map/ppermute | solution.py:50
  28.5 20.2 %all-reduce.3 = (f32[1,16]{1,0:T(1,128)S(1)}, f32[1,16]{1,0:T(1,128)S(1)}) all-reduce(f32[1,16]{1,0:T(1,128)S(1)} %multiply_bitcast_fusion.2, f32[1,16]{1,0:T(1,128)S(1)} %fusion.33), channel_id=1, replica_groups=mesh['tier'=4,'tile'=8] {'tile'}, use_global_device_ids=true, to_apply=%region_4.5 | all-reduce | flops 32 | bytes 256 | tf_op jit(solution)/shard_map/psum | solution.py:121
  49.7 1.2 fusion.18
  51.2 0.9 copy.27
  52.0 3.6 %reshape.186 = f32[4,1,24576]{2,1,0:T(1,128)} reshape(f32[1024,4,24]{2,1,0:T(4,128)S(1)} %bitcast.146) | data formatting | bytes 786432
  55.7 3.5 %all-to-all-start = ((f32[4,1,24576]{2,1,0:T(1,128)}), f32[4,1,24576]{2,1,0:T(1,128)S(1)}, u32[]{:S(2)}, u32[]{:S(2)}) async-start(f32[4,1,24576]{2,1,0:T(1,128)} %reshape.186), calls=%async_computation | async-start | bytes 786432 | tf_op jit(solution)/shard_map/all_to_all | solution.py:163
  59.2 7.4 %all-to-all-done = f32[4,1,24576]{2,1,0:T(1,128)S(1)} async-done(((f32[4,1,24576]{2,1,0:T(1,128)}), f32[4,1,24576]{2,1,0:T(1,128)S(1)}, u32[]{:S(2)}, u32[]{:S(2)}) %all-to-all-start) | async-done | bytes 393248 | tf_op jit(solution)/shard_map/all_to_all | solution.py:163
  67.0 1.7 %reduce.10 = f32[4,24576]{1,0:T(4,128)S(1)} reduce(f32[4,1,24576]{2,1,0:T(1,128)S(1)} %all-to-all-done, f32[]{:T(128)} %broadcast.194), dimensions={1}, to_apply=%all_to_all.26.reduce_sub_computation | reduce | bytes 786436 | tf_op jit(solution)/shard_map/all_to_all | solution.py:163
  68.7 2.8 %reshape.187 = f32[1024,4,24]{2,1,0:T(4,128)S(1)} reshape(f32[4,24576]{1,0:T(4,128)S(1)} %reduce.10) | data formatting | bytes 786432
  71.5 0.8 copy.28
  73.3 1.4 %collective-permute-start.6 = (f32[4,24,256]{2,1,0:T(8,128)S(1)}, f32[4,24,256]{2,1,0:T(8,128)S(1)}, u32[]{:S(2)}, u32[]{:S(2)}) collective-permute-start(f32[4,24,256]{2,1,0:T(8,128)S(1)} %get-tuple-element.49), channel_id=1, source_target_pairs={{0,24},{8,16},{16,8},{24,0},{1,25},{9,17},{17,9},{25,1},{2,26},{10... | collective-permute-start | bytes 294920 | tf_op jit(solution)/shard_map/ppermute | solution.py:37
  74.7 3.8 %collective-permute-done.5 = f32[4,24,256]{2,1,0:T(8,128)S(1)} collective-permute-done((f32[4,24,256]{2,1,0:T(8,128)S(1)}, f32[4,24,256]{2,1,0:T(8,128)S(1)}, u32[]{:S(2)}, u32[]{:S(2)}) %collective-permute-start.5) | collective-permute-done | bytes 98336 | tf_op jit(solution)/shard_map/ppermute | solution.py:37
  78.5 1.2 collective-permute-done.6
  80.4 1.4 %collective-permute-start.7 = (f32[1,24,1024]{2,1,0:T(8,128)S(1)}, f32[1,24,1024]{2,1,0:T(8,128)S(1)}, u32[]{:S(2)}, u32[]{:S(2)}) collective-permute-start(f32[1,24,1024]{2,1,0:T(8,128)S(1)} %bitcast.167), channel_id=1, source_target_pairs={{1,0},{2,1},{3,2},{4,3},{5,4},{6,5},{7,6},{9,8},{10,9},{11,10},{12... | collective-permute-start | bytes 294920 | tf_op jit(solution)/shard_map/ppermute | solution.py:53
  82.2 4.5 %collective-permute-start.8 = (f32[1,24,1024]{2,1,0:T(8,128)S(1)}, f32[1,24,1024]{2,1,0:T(8,128)S(1)}, u32[]{:S(2)}, u32[]{:S(2)}) collective-permute-start(f32[1,24,1024]{2,1,0:T(8,128)S(1)} %bitcast.168), channel_id=1, source_target_pairs={{0,1},{1,2},{2,3},{3,4},{4,5},{5,6},{6,7},{8,9},{9,10},{10,11},{11... | collective-permute-start | bytes 294920 | tf_op jit(solution)/shard_map/ppermute | solution.py:50
  86.8 17.1 %psum.26 = f32[1,16]{1,0:T(1,128)S(1)} all-reduce(f32[1,16]{1,0:T(1,128)S(1)} %fusion.32), channel_id=1, replica_groups=mesh['tier'=4,'tile'=8] {'tile'}, use_global_device_ids=true, to_apply=%region_7.8 | all-reduce | flops 16 | bytes 128 | tf_op jit(solution)/shard_map/psum | solution.py:121
  104.4 1.4 %fusion.7 = f32[4,24,1024]{2,1,0:T(8,128)S(1)} fusion(f32[4,24,1024]{2,1,0:T(8,128)S(1)} %bitcast.152, f32[6,24,1026]{2,1,0:T(8,128)S(1)} %select_maximum_fusion.3, f32[4,24,1024]{2,1,0:T(8,128)} %get-tuple-element.30, f32[1,24,1024]{2,1,0:T(8,128)S(1)} %collective-permute-done.8, f32[4,24,1024]{2,1,0:T(8,128)S(1)} %get-tuple-element.29, ...), kind=kLoop, calls=%fused_computation.23 | loop fusion | flops 2162688 | bytes 3735552 | tf_op jit(solution)/shard_map/add | solution.py:78
  106.2 0.9 copy.32
  107.1 2.9 %reshape.188 = f32[4,1,24576]{2,1,0:T(1,128)S(1)} reshape(f32[1024,4,24]{2,1,0:T(4,128)S(1)} %bitcast.148) | data formatting | bytes 786432
  110.0 9.8 %all_to_all.36 = f32[4,1,24576]{2,1,0:T(1,128)S(1)} all-to-all(f32[4,1,24576]{2,1,0:T(1,128)S(1)} %reshape.188), channel_id=1, replica_groups=mesh['tier'=4,'tile'=8] {'tier'}, dimensions={0} | all-to-all | bytes 786432 | tf_op jit(solution)/shard_map/all_to_all | solution.py:163
  119.8 1.7 %reduce.11 = f32[4,24576]{1,0:T(4,128)S(1)} reduce(f32[4,1,24576]{2,1,0:T(1,128)S(1)} %all_to_all.36, f32[]{:T(128)} %broadcast.194), dimensions={1}, to_apply=%all_to_all.30.reduce_sub_computation | reduce | bytes 786436 | tf_op jit(solution)/shard_map/all_to_all | solution.py:163
  121.4 2.8 %reshape.189 = f32[1024,4,24]{2,1,0:T(4,128)S(1)} reshape(f32[4,24576]{1,0:T(4,128)S(1)} %reduce.11) | data formatting | bytes 786432
  126.1 1.4 %collective-permute-start.11 = (f32[4,24,256]{2,1,0:T(8,128)S(1)}, f32[4,24,256]{2,1,0:T(8,128)S(1)}, u32[]{:S(2)}, u32[]{:S(2)}) collective-permute-start(f32[4,24,256]{2,1,0:T(8,128)S(1)} %get-tuple-element.43), channel_id=1, source_target_pairs={{0,24},{8,16},{16,8},{24,0},{1,25},{9,17},{17,9},{25,1},{2,26},{10... | collective-permute-start | bytes 294920 | tf_op jit(solution)/shard_map/ppermute | solution.py:37
  127.5 3.8 %collective-permute-done.10 = f32[4,24,256]{2,1,0:T(8,128)S(1)} collective-permute-done((f32[4,24,256]{2,1,0:T(8,128)S(1)}, f32[4,24,256]{2,1,0:T(8,128)S(1)}, u32[]{:S(2)}, u32[]{:S(2)}) %collective-permute-start.10) | collective-permute-done | bytes 98336 | tf_op jit(solution)/shard_map/ppermute | solution.py:37
  131.3 1.2 collective-permute-done.11
  133.1 0.8 copy.38
  (66 shorter events, 7.3 us)
Async XLA Ops:
  0.6 71.6 %copy-start = (f32[96,96]{1,0:T(8,128)S(1)}, f32[96,96]{1,0:T(8,128)}, u32[]{:S(2)}) copy-start(f32[96,96]{1,0:T(8,128)} %param.17) | copy-start | bytes 110596
  9.1 12.2 %copy-start.3 = (f32[4,24,1024]{2,1,0:T(8,128)S(1)}, f32[4,24,1024]{2,1,0:T(8,128)}, u32[]{:S(2)}) copy-start(f32[4,24,1024]{2,1,0:T(8,128)} %param.11) | copy-start | bytes 1179652
  9.1 19.1 %copy-start.7 = (s32[1,8]{1,0:T(1,128)S(1)}, s32[1,8]{1,0:T(1,128)}, u32[]{:S(2)}) copy-start(s32[1,8]{1,0:T(1,128)} %param.14) | copy-start | bytes 100
  9.1 39.7 %copy-start.5 = (f32[4,16]{1,0:T(4,128)S(1)}, f32[4,16]{1,0:T(4,128)}, u32[]{:S(2)}) copy-start(f32[4,16]{1,0:T(4,128)} %param.15) | copy-start | bytes 772
  9.1 39.7 %copy-start.6 = (f32[4,16]{1,0:T(4,128)S(1)}, f32[4,16]{1,0:T(4,128)}, u32[]{:S(2)}) copy-start(f32[4,16]{1,0:T(4,128)} %param.16) | copy-start | bytes 772
  14.5 34.8 %collective-permute-start = (f32[2,1,24,1024]{3,2,1,0:T(8,128)S(1)}, f32[2,1,24,1024]{3,2,1,0:T(8,128)S(1)}, u32[]{:S(2)}, u32[]{:S(2)}) collective-permute-start(f32[2,1,24,1024]{3,2,1,0:T(8,128)S(1)} %get-tuple-element.41), channel_id=1, source_target_pairs={{1,0},{2,1},{3,2},{4,3},{5,4},{6,5},{7,6},{9,8},{10,9},{11,10},{12... | collective-permute-start | bytes 589832 | tf_op jit(solution)/shard_map/ppermute | solution.py:53
  15.8 33.5 %collective-permute-start.2 = (f32[2,1,24,1024]{3,2,1,0:T(8,128)S(1)}, f32[2,1,24,1024]{3,2,1,0:T(8,128)S(1)}, u32[]{:S(2)}, u32[]{:S(2)}) collective-permute-start(f32[2,1,24,1024]{3,2,1,0:T(8,128)S(1)} %get-tuple-element.40), channel_id=1, source_target_pairs={{0,1},{1,2},{2,3},{3,4},{4,5},{5,6},{6,7},{8,9},{9,10},{10,11},{11... | collective-permute-start | bytes 589832 | tf_op jit(solution)/shard_map/ppermute | solution.py:50
  21.4 27.7 %collective-permute-start.1 = (f32[1,24,1024]{2,1,0:T(8,128)S(1)}, f32[1,24,1024]{2,1,0:T(8,128)S(1)}, u32[]{:S(2)}, u32[]{:S(2)}) collective-permute-start(f32[1,24,1024]{2,1,0:T(8,128)S(1)} %get-tuple-element.53), channel_id=1, source_target_pairs={{1,0},{2,1},{3,2},{4,3},{5,4},{6,5},{7,6},{9,8},{10,9},{11,10},{12... | collective-permute-start | bytes 294920 | tf_op jit(solution)/shard_map/ppermute | solution.py:53
  22.7 26.4 %collective-permute-start.3 = (f32[1,24,1024]{2,1,0:T(8,128)S(1)}, f32[1,24,1024]{2,1,0:T(8,128)S(1)}, u32[]{:S(2)}, u32[]{:S(2)}) collective-permute-start(f32[1,24,1024]{2,1,0:T(8,128)S(1)} %get-tuple-element.52), channel_id=1, source_target_pairs={{0,1},{1,2},{2,3},{3,4},{4,5},{5,6},{6,7},{8,9},{9,10},{10,11},{11... | collective-permute-start | bytes 294920 | tf_op jit(solution)/shard_map/ppermute | solution.py:50
  49.7 1.3 copy-start.1
  55.7 10.9 %all-to-all-start = ((f32[4,1,24576]{2,1,0:T(1,128)}), f32[4,1,24576]{2,1,0:T(1,128)S(1)}, u32[]{:S(2)}, u32[]{:S(2)}) async-start(f32[4,1,24576]{2,1,0:T(1,128)} %reshape.186), calls=%async_computation | async-start | bytes 786432 | tf_op jit(solution)/shard_map/all_to_all | solution.py:163
  72.8 1.9 %collective-permute-start.4 = (f32[4,24,256]{2,1,0:T(8,128)S(1)}, f32[4,24,256]{2,1,0:T(8,128)S(1)}, u32[]{:S(2)}, u32[]{:S(2)}) collective-permute-start(f32[4,24,256]{2,1,0:T(8,128)S(1)} %get-tuple-element.51), channel_id=1, source_target_pairs={{0,8},{8,0},{16,24},{24,16},{1,9},{9,1},{17,25},{25,17},{2,10},{10... | collective-permute-start | bytes 294920 | tf_op jit(solution)/shard_map/ppermute | solution.py:37
  72.9 5.7 %collective-permute-start.5 = (f32[4,24,256]{2,1,0:T(8,128)S(1)}, f32[4,24,256]{2,1,0:T(8,128)S(1)}, u32[]{:S(2)}, u32[]{:S(2)}) collective-permute-start(f32[4,24,256]{2,1,0:T(8,128)S(1)} %get-tuple-element.50), channel_id=1, source_target_pairs={{0,16},{8,24},{16,0},{24,8},{1,17},{9,25},{17,1},{25,9},{2,18},{10... | collective-permute-start | bytes 294920 | tf_op jit(solution)/shard_map/ppermute | solution.py:37
  73.3 6.4 %collective-permute-start.6 = (f32[4,24,256]{2,1,0:T(8,128)S(1)}, f32[4,24,256]{2,1,0:T(8,128)S(1)}, u32[]{:S(2)}, u32[]{:S(2)}) collective-permute-start(f32[4,24,256]{2,1,0:T(8,128)S(1)} %get-tuple-element.49), channel_id=1, source_target_pairs={{0,24},{8,16},{16,8},{24,0},{1,25},{9,17},{17,9},{25,1},{2,26},{10... | collective-permute-start | bytes 294920 | tf_op jit(solution)/shard_map/ppermute | solution.py:37
  80.4 24.1 %copy-start.2 = (f32[2,6,24,1026]{3,2,1,0:T(8,128)S(1)}, f32[2,6,24,1026]{3,2,1,0:T(8,128)}, u32[]{:S(2)}) copy-start(f32[2,6,24,1026]{3,2,1,0:T(8,128)} %copy-done.1) | copy-start | bytes 3545860
  80.4 23.8 %collective-permute-start.7 = (f32[1,24,1024]{2,1,0:T(8,128)S(1)}, f32[1,24,1024]{2,1,0:T(8,128)S(1)}, u32[]{:S(2)}, u32[]{:S(2)}) collective-permute-start(f32[1,24,1024]{2,1,0:T(8,128)S(1)} %bitcast.167), channel_id=1, source_target_pairs={{1,0},{2,1},{3,2},{4,3},{5,4},{6,5},{7,6},{9,8},{10,9},{11,10},{12... | collective-permute-start | bytes 294920 | tf_op jit(solution)/shard_map/ppermute | solution.py:53
  82.2 22.0 %collective-permute-start.8 = (f32[1,24,1024]{2,1,0:T(8,128)S(1)}, f32[1,24,1024]{2,1,0:T(8,128)S(1)}, u32[]{:S(2)}, u32[]{:S(2)}) collective-permute-start(f32[1,24,1024]{2,1,0:T(8,128)S(1)} %bitcast.168), channel_id=1, source_target_pairs={{0,1},{1,2},{2,3},{3,4},{4,5},{5,6},{6,7},{8,9},{9,10},{10,11},{11... | collective-permute-start | bytes 294920 | tf_op jit(solution)/shard_map/ppermute | solution.py:50
  103.9 1.9 %copy-start.4 = (f32[1,16]{1,0:T(1,128)}, f32[1,16]{1,0:T(1,128)S(1)}, u32[]{:S(2)}) copy-start(f32[1,16]{1,0:T(1,128)S(1)} %exponential_multiply_fusion) | copy-start | bytes 196
  125.6 1.9 %collective-permute-start.9 = (f32[4,24,256]{2,1,0:T(8,128)S(1)}, f32[4,24,256]{2,1,0:T(8,128)S(1)}, u32[]{:S(2)}, u32[]{:S(2)}) collective-permute-start(f32[4,24,256]{2,1,0:T(8,128)S(1)} %get-tuple-element.45), channel_id=1, source_target_pairs={{0,8},{8,0},{16,24},{24,16},{1,9},{9,1},{17,25},{25,17},{2,10},{10... | collective-permute-start | bytes 294920 | tf_op jit(solution)/shard_map/ppermute | solution.py:37
  125.6 5.7 %collective-permute-start.10 = (f32[4,24,256]{2,1,0:T(8,128)S(1)}, f32[4,24,256]{2,1,0:T(8,128)S(1)}, u32[]{:S(2)}, u32[]{:S(2)}) collective-permute-start(f32[4,24,256]{2,1,0:T(8,128)S(1)} %get-tuple-element.44), channel_id=1, source_target_pairs={{0,16},{8,24},{16,0},{24,8},{1,17},{9,25},{17,1},{25,9},{2,18},{10... | collective-permute-start | bytes 294920 | tf_op jit(solution)/shard_map/ppermute | solution.py:37
  126.1 6.4 %collective-permute-start.11 = (f32[4,24,256]{2,1,0:T(8,128)S(1)}, f32[4,24,256]{2,1,0:T(8,128)S(1)}, u32[]{:S(2)}, u32[]{:S(2)}) collective-permute-start(f32[4,24,256]{2,1,0:T(8,128)S(1)} %get-tuple-element.43), channel_id=1, source_target_pairs={{0,24},{8,16},{16,8},{24,0},{1,25},{9,17},{17,9},{25,1},{2,26},{10... | collective-permute-start | bytes 294920 | tf_op jit(solution)/shard_map/ppermute | solution.py:37
